TPU v7x, 256 devices: a whole 4x4x8 slice. The times are simulated.
256 devices in a mesh: seg: 16 (over z, core), bond: 16 (over x, y).
Axes of the slice: x: 4, y: 4, z: 8, core: 2. Of those that a mesh axis runs over, the one named last changes fastest.
Arguments:
- left_env: bfloat16 [16, 1024, 6, 1024], P('seg', 'bond'), may hold values from -0.1875 to 0.1875
- prev_left: bfloat16 [16, 1024, 1024], P('seg'), may hold values from -0.25 to 1.25
- cur_site: bfloat16 [16, 1024, 4, 1024], P('seg', 'bond'), may hold values from -6 to 6
- prev_site: bfloat16 [16, 1024, 4, 1024], P('seg', None, None, 'bond'), may hold values from -6 to 6
- hamiltonian: bfloat16 [16, 6, 6, 4, 4], P('seg'), may hold values from -1.25 to 1.25
- right_env: bfloat16 [16, 1024, 6, 1024], P('seg', 'bond'), may hold values from -0.078125 to 0.078125
- prev_right: bfloat16 [16, 1024, 1024], P('seg'), may hold values from -0.25 to 1.25
Outputs:
- new_site: bfloat16 [16, 1024, 4, 1024], P('seg', 'bond')
- center: float32 [16, 1024, 1024], P('seg', 'bond')
All inputs are finite; a program needn't handle non-finite values.
Results may differ from a plain program's by a relative error of at most 0.0054.
Values may be sent and summed in bfloat16 or wider, within the bound.
No kernel may reach another device: no remote copies, remote signals or barrier semaphores. Data moves between devices by JAX's collectives and lax.ppermute only.
A program may use at most 128 MiB of HBM per device.

v0:
```python
import math
import jax
import jax.numpy as jnp
from jax import lax
from jax.sharding import PartitionSpec as P

PHYS = 4
MPOB = 6


def shifted(block, axis, distance):
    devices = range(lax.axis_size(axis))
    route = [((i - distance) % len(devices), i) for i in devices]
    return lax.ppermute(block, axis, route)


def shards(left_env, prev_left, cur_site, prev_site, hamiltonian, right_env, prev_right):
    left_now, prev_now = shifted((left_env[0], prev_left[0]), "seg", 1)
    own_rows = left_now.shape[0]
    bond_width = left_now.shape[2]
    coupling = hamiltonian[0].astype(jnp.float32)
    current = lax.all_gather(cur_site[0], "bond", axis=0, tiled=True)
    projected = jnp.dot(
        left_now.reshape(own_rows * MPOB, bond_width),
        current.reshape(bond_width, PHYS * bond_width),
        preferred_element_type=jnp.float32,
    ).reshape(own_rows, MPOB, PHYS, bond_width)
    mixture = jnp.einsum(
        "autc,uvst->asvc", projected, coupling, precision=lax.Precision.HIGHEST
    ).astype(jnp.bfloat16)
    applied = jnp.einsum(
        "asvc,cvy->asy",
        mixture,
        lax.all_gather(right_env[0], "bond", axis=0, tiled=True),
        preferred_element_type=jnp.float32,
    )
    previous = lax.all_gather(prev_site[0], "bond", axis=2, tiled=True)
    own_left = lax.dynamic_slice_in_dim(prev_now, lax.axis_index("bond") * own_rows, own_rows, 0)
    partial_value = jnp.einsum(
        "ab,bsc->asc", own_left, previous, preferred_element_type=jnp.float32
    ).astype(jnp.bfloat16)
    second = jnp.einsum(
        "asc,cy->asy", partial_value, prev_right[0], preferred_element_type=jnp.float32
    )
    target = (2.0 * applied - second).reshape(own_rows * PHYS, bond_width)
    local_correlation = jnp.dot(
        target.T, target, precision=lax.Precision.HIGHEST, preferred_element_type=jnp.float32
    )
    correlation = lax.psum(local_correlation, "bond")
    triangle = jnp.linalg.cholesky(correlation)
    solved = jax.scipy.linalg.solve_triangular(triangle, target.T, lower=True)
    norming = math.sqrt(bond_width * PHYS)
    new_site = (solved.T * norming).astype(jnp.bfloat16).reshape(1, own_rows, PHYS, bond_width)
    offset = lax.axis_index("bond") * own_rows
    center = lax.dynamic_slice_in_dim(triangle.T, offset, own_rows, 0) / norming
    return (new_site, center[None])


def solution(mesh):
    return jax.shard_map(
        shards,
        mesh=mesh,
        in_specs=(
            P("seg", "bond", None, None),
            P("seg", None, None),
            P("seg", "bond", None, None),
            P("seg", None, None, "bond"),
            P("seg", None, None, None, None),
            P("seg", "bond", None, None),
            P("seg", None, None),
        ),
        out_specs=(P("seg", "bond", None, None), P("seg", "bond", None)),
        check_vma=False,
    )
```

profile of v0, /device:TPU:1, one launch (start us, length us, event | category | flops | bytes accessed | tf_op | source)
XLA Modules:
  0.0 756.7 jit_solution(14787921494383537855)
XLA Ops:
  11.0 3.0 collective-permute-start
  14.1 75.9 %all-gather.7.cloned.1.call-done = bf16[1,1024,4,1024]{3,2,0,1:T(4,128)(2,1)} async-done(((bf16[1,64,4,1024]{3,2,0,1:T(4,128)(2,1)}), bf16[1,1024,4,1024]{3,2,0,1:T(4,128)(2,1)}) %all-gather.7.cloned.1.call-update) | async-done | bytes 8388624 | tf_op jit(solution)/shard_map/all_gather | solution.py:22
  90.0 13.8 %copy.82 = bf16[1,1024,4,1024]{1,3,2,0:T(8,128)(2,1)} copy(bf16[1,1024,4,1024]{3,2,0,1:T(4,128)(2,1)} %all-gather.7.cloned.1.call-done) | data formatting | bytes 16777216 | tf_op jit(solution)/shard_map/reshape | solution.py:25
  103.9 64.7 %all-gather.11.cloned.1.call-done = bf16[1,1024,4,1024]{1,2,0,3:T(4,128)(2,1)} async-done(((bf16[1,1024,4,64]{1,2,0,3:T(4,128)(2,1)}), bf16[1,1024,4,1024]{1,2,0,3:T(4,128)(2,1)}) %all-gather.11.cloned.1.call-update) | async-done | bytes 8388624 | tf_op jit(solution)/shard_map/all_gather | solution.py:37
  168.6 13.7 %copy.57 = bf16[1,1024,4,1024]{3,1,2,0:T(8,128)(2,1)} copy(bf16[1,1024,4,1024]{1,2,0,3:T(4,128)(2,1)} %all-gather.11.cloned.1.call-done) | data formatting | bytes 16777216 | tf_op jit(solution)/shard_map/all_gather | solution.py:37
  182.3 6.3 fusion.14
  188.6 11.5 %fusion.8 = bf16[64,4,6,1024]{3,2,1,0:T(8,128)(2,1)} fusion(f32[64,6,4,1024,1]{3,0,2,1,4:T(8,128)S(1)} %fusion.14, bf16[1,6,6,4,4]{2,4,3,1,0:T(4,128)(2,1)S(1)} %copy-done.4), kind=kOutput, calls=%fused_computation.11 | convolution fusion | flops 454557696 | bytes 9438336 | tf_op jit(solution)/shard_map/autc,uvst->asvc/dot_general | solution.py:28
  200.2 65.7 %all-gather.9.cloned.1.call-done = bf16[1,1024,6,1024]{3,1,2,0:T(8,128)(2,1)} async-done(((bf16[1,64,6,1024]{3,1,2,0:T(8,128)(2,1)}), bf16[1,1024,6,1024]{3,1,2,0:T(8,128)(2,1)}) %all-gather.9.cloned.1.call-update) | async-done | bytes 12582928 | tf_op jit(solution)/shard_map/all_gather | solution.py:34
  265.9 12.8 %fusion.24 = f32[64,4,1024]{2,0,1:T(8,128)} fusion(bf16[1,1024,6,1024]{3,1,2,0:T(8,128)(2,1)} %all-gather.9.cloned.1.call-done, bf16[64,4,6,1024]{3,2,1,0:T(8,128)(2,1)} %fusion.8), kind=kOutput, calls=%fused_computation.23 | convolution fusion | flops 3221487616 | bytes 16777216 | tf_op jit(solution)/shard_map/asvc,cvy->asy/dot_general | solution.py:31
  278.7 5.8 fusion.29
  284.5 5.1 convolution_bitcast_fusion
  291.1 111.9 %all-reduce.3.cloned.1.call-done = f32[1024,1024]{0,1:T(8,128)} async-done(((f32[1024,1024]{0,1:T(8,128)}), f32[1024,1024]{0,1:T(8,128)}) %all-reduce.3.cloned.1.call-update) | async-done | bytes 4194320 | tf_op jit(solution)/shard_map/psum | solution.py:49
  403.0 5.5 copy.59
  408.5 4.4 fusion.9
  414.9 11.7 %cholesky.223 = f32[128,128]{1,0:T(8,128)S(1)} custom-call(f32[128,128]{1,0:T(8,128)S(1)} %cholesky.580), custom_call_target="Cholesky" | custom-call | tf_op jit(solution)/shard_map/jit(cholesky)/cholesky | solution.py:50
  426.6 9.8 %custom-call.63 = f32[1,128,128]{1,2,0:T(8,128)S(1)} custom-call(f32[1,128,128]{2,1,0:T(8,128)S(1)} %get-tuple-element.76), custom_call_target="InvertDiagBlocksLowerTriangular" | custom-call | tf_op jit(solution)/shard_map/jit(cholesky)/cholesky | solution.py:50
  442.7 11.9 %cholesky.244 = f32[128,128]{1,0:T(8,128)S(1)} custom-call(f32[128,128]{1,0:T(8,128)S(1)} %cholesky.584), custom_call_target="Cholesky" | custom-call | tf_op jit(solution)/shard_map/jit(cholesky)/cholesky | solution.py:50
  456.1 9.8 %custom-call.64 = f32[1,128,128]{1,2,0:T(8,128)S(1)} custom-call(f32[1,128,128]{2,1,0:T(8,128)S(1)} %get-tuple-element.73), custom_call_target="InvertDiagBlocksLowerTriangular" | custom-call | tf_op jit(solution)/shard_map/jit(cholesky)/cholesky | solution.py:50
  469.3 11.7 %cholesky.468 = f32[128,128]{1,0:T(8,128)S(1)} custom-call(f32[128,128]{1,0:T(8,128)S(1)} %cholesky.589), custom_call_target="Cholesky" | custom-call | tf_op jit(solution)/shard_map/jit(cholesky)/cholesky | solution.py:50
  482.3 9.8 %custom-call.65 = f32[1,128,128]{1,2,0:T(8,128)S(1)} custom-call(f32[1,128,128]{2,1,0:T(8,128)S(1)} %get-tuple-element.70), custom_call_target="InvertDiagBlocksLowerTriangular" | custom-call | tf_op jit(solution)/shard_map/jit(cholesky)/cholesky | solution.py:50
  495.6 12.1 %cholesky.487 = f32[128,128]{1,0:T(8,128)S(1)} custom-call(f32[128,128]{1,0:T(8,128)S(1)} %cholesky.594), custom_call_target="Cholesky" | custom-call | tf_op jit(solution)/shard_map/jit(cholesky)/cholesky | solution.py:50
  509.0 9.8 %custom-call.66 = f32[1,128,128]{1,2,0:T(8,128)S(1)} custom-call(f32[1,128,128]{2,1,0:T(8,128)S(1)} %get-tuple-element.67), custom_call_target="InvertDiagBlocksLowerTriangular" | custom-call | tf_op jit(solution)/shard_map/jit(cholesky)/cholesky | solution.py:50
  522.3 11.7 %cholesky.506 = f32[128,128]{1,0:T(8,128)S(1)} custom-call(f32[128,128]{1,0:T(8,128)S(1)} %cholesky.599), custom_call_target="Cholesky" | custom-call | tf_op jit(solution)/shard_map/jit(cholesky)/cholesky | solution.py:50
  535.4 10.0 %custom-call.67 = f32[1,128,128]{1,2,0:T(8,128)S(1)} custom-call(f32[1,128,128]{2,1,0:T(8,128)S(1)} %get-tuple-element.64), custom_call_target="InvertDiagBlocksLowerTriangular" | custom-call | tf_op jit(solution)/shard_map/jit(cholesky)/cholesky | solution.py:50
  548.7 11.7 %cholesky.526 = f32[128,128]{1,0:T(8,128)S(1)} custom-call(f32[128,128]{1,0:T(8,128)S(1)} %cholesky.604), custom_call_target="Cholesky" | custom-call | tf_op jit(solution)/shard_map/jit(cholesky)/cholesky | solution.py:50
  561.7 9.8 %custom-call.68 = f32[1,128,128]{1,2,0:T(8,128)S(1)} custom-call(f32[1,128,128]{2,1,0:T(8,128)S(1)} %get-tuple-element.61), custom_call_target="InvertDiagBlocksLowerTriangular" | custom-call | tf_op jit(solution)/shard_map/jit(cholesky)/cholesky | solution.py:50
  574.5 11.9 %cholesky.546 = f32[128,128]{1,0:T(8,128)S(1)} custom-call(f32[128,128]{1,0:T(8,128)S(1)} %cholesky.609), custom_call_target="Cholesky" | custom-call | tf_op jit(solution)/shard_map/jit(cholesky)/cholesky | solution.py:50
  587.6 9.8 %custom-call.69 = f32[1,128,128]{1,2,0:T(8,128)S(1)} custom-call(f32[1,128,128]{2,1,0:T(8,128)S(1)} %get-tuple-element.58), custom_call_target="InvertDiagBlocksLowerTriangular" | custom-call | tf_op jit(solution)/shard_map/jit(cholesky)/cholesky | solution.py:50
  600.1 11.7 %cholesky.564 = f32[128,128]{1,0:T(8,128)S(1)} custom-call(f32[128,128]{1,0:T(8,128)S(1)} %convolution_subtract_fusion.13), custom_call_target="Cholesky" | custom-call | tf_op jit(solution)/shard_map/jit(cholesky)/cholesky | solution.py:50
  618.8 6.6 fusion.10
  625.3 27.4 %while.1 = (s32[]{:T(128)}, f32[1024,1024]{1,0:T(8,128)}, s32[8,2]{0,1:T(2,128)S(1)}, f32[8,128,128]{2,1,0:T(8,128)}, s32[]{:T(128)}) while((s32[]{:T(128)}, f32[1024,1024]{1,0:T(8,128)}, s32[8,2]{0,1:T(2,128)S(1)}, f32[8,128,128]{2,1,0:T(8,128)}, s32[]{:T(128)}) %tuple.65), condition=%wide.while_cond, body=%wide.while_body.sunk | while | flops 2 | bytes 132705 | solution.py:51
  652.7 79.6 %custom-call.70 = f32[8,128,128]{1,2,0:T(8,128)S(1)} custom-call(f32[8,128,128]{2,1,0:T(8,128)} %get-tuple-element.9), custom_call_target="InvertDiagBlocksLowerTriangular" | custom-call | tf_op jit(solution)/shard_map/jit(_solve_triangular)/triangular_solve | solution.py:51
  (111 shorter events, 87.4 us)
Async XLA Ops:
  7.2 271.5 %copy-start = (bf16[1,1024,1024]{2,1,0:T(8,128)(2,1)S(1)}, bf16[1,1024,1024]{2,1,0:T(8,128)(2,1)}, u32[]{:S(2)}) copy-start(bf16[1,1024,1024]{2,1,0:T(8,128)(2,1)} %param.13) | copy-start | bytes 6291460
  7.2 82.9 %all-gather.7.cloned.1.call-start = ((), (), s32[]{:S(2)}) async-start(), calls=%async_computation.1 | async-start | bytes 8912896 | tf_op jit(solution)/shard_map/all_gather | solution.py:22
  7.9 160.7 %all-gather.11.cloned.1.call-start = ((), (), s32[]{:S(2)}) async-start(), calls=%async_computation.3 | async-start | bytes 8912896 | tf_op jit(solution)/shard_map/all_gather | solution.py:37
  10.2 255.6 %all-gather.9.cloned.1.call-start = ((), (), s32[]{:S(2)}) async-start(), calls=%async_computation.2 | async-start | bytes 13369344 | tf_op jit(solution)/shard_map/all_gather | solution.py:34
  11.0 392.0 %all-reduce.3.cloned.1.call-start = ((), (), s32[]{:S(2)}) async-start(), calls=%async_computation | async-start | bytes 8388608 | tf_op jit(solution)/shard_map/psum | solution.py:49
  11.0 171.3 %collective-permute-start = (bf16[64,6,1024]{2,0,1:T(8,128)(2,1)}, bf16[64,6,1024]{2,0,1:T(8,128)(2,1)S(1)}, u32[]{:S(2)}, u32[]{:S(2)}) collective-permute-start(bf16[64,6,1024]{2,0,1:T(8,128)(2,1)} %bitcast.185), channel_id=1, source_target_pairs={{240,0},{0,16},{16,32},{32,48},{48,64},{64,80},{80,96},{96,112},{1... | collective-permute-start | bytes 2359304 | tf_op jit(solution)/shard_map/ppermute | solution.py:14
  14.1 264.6 %collective-permute-start.1 = (bf16[1024,1024]{1,0:T(8,128)(2,1)}, bf16[1024,1024]{1,0:T(8,128)(2,1)}, u32[]{:S(2)}, u32[]{:S(2)}) collective-permute-start(bf16[1024,1024]{1,0:T(8,128)(2,1)} %bitcast.184), channel_id=1, source_target_pairs={{240,0},{0,16},{16,32},{32,48},{48,64},{64,80},{80,96},{96,112},{1... | collective-permute-start | bytes 6291464 | tf_op jit(solution)/shard_map/ppermute | solution.py:14
  182.3 6.3 copy-start.4
  412.9 1.9 copy-start.2
  732.3 8.1 %copy-start.3 = (f32[8,128,128]{1,2,0:T(8,128)}, f32[8,128,128]{1,2,0:T(8,128)S(1)}, u32[]{:S(2)}) copy-start(f32[8,128,128]{1,2,0:T(8,128)S(1)} %custom-call.70) | copy-start | bytes 1572868
  740.8 9.1 %copy-start.1 = (bf16[1,1024,1024]{2,1,0:T(8,128)(2,1)S(1)}, bf16[1,1024,1024]{2,1,0:T(8,128)(2,1)}, u32[]{:S(2)}) copy-start(bf16[1,1024,1024]{2,1,0:T(8,128)(2,1)} %param.13) | copy-start | bytes 6291460
Sparse Core Ops, SparseCore 0:
  10.4 79.5 all-gather.6
  93.0 75.4 all-gather.10
  171.1 94.7 all-gather.8
  289.8 113.1 all-reduce.2
where the time goes:
time: 764 us; the launch traced here: 757 us
  waiting for transfers between devices  320 us (42%)
  other arithmetic  264 us (35%)
  matrix products  78.2 us (10%)
  local copies, waits for them, and re-layouts  71.6 us (9%)
  between operations  19.4 us (3%)
    another operation x30, other arithmetic, shards(): triangle = jnp.linalg.cholesky(correlation)  172 us
    psum x1, waiting for transfers between devices, shards(): correlation = lax.psum(local_correlation, 'bond')  112 us
    another operation x3, other arithmetic, shards(): solved = jax.scipy.linalg.solve_triangular(triangle, target.T, lower=True)  86.2 us
    all_gather x1, waiting for transfers between devices, shards(): current = lax.all_gather(cur_site[0], 'bond', axis=0, tiled=True)  75.9 us
    all_gather x1, waiting for transfers between devices, shards(): lax.all_gather(right_env[0], 'bond', axis=0, tiled=True)  65.7 us
    all_gather x1, waiting for transfers between devices, shards(): previous = lax.all_gather(prev_site[0], 'bond', axis=2, tiled=True)  64.7 us
    another operation x24, local copies, waits for them, and re-layouts  27.4 us
    another operation x14, matrix products, shards(): triangle = jnp.linalg.cholesky(correlation)  22.7 us
  transfers between devices with their start and end apart: 6, of which 4 were waited for; matrix products, arithmetic and copies ran while one was open for 8% of the time, Pallas kernels for 0%

commit v1 on v0

--- a/solution.py
+++ b/solution.py
@@ -31,7 +31,9 @@
     applied = jnp.einsum(
         "asvc,cvy->asy",
         mixture,
-        lax.all_gather(right_env[0], "bond", axis=0, tiled=True),
+        jnp.concatenate(
+            lax.all_to_all(jnp.stack([right_env[0]] * lax.axis_size("bond")), "bond", 0, 0), axis=0
+        ),
         preferred_element_type=jnp.float32,
     )
     previous = lax.all_gather(prev_site[0], "bond", axis=2, tiled=True)

time: 764 us -> 893 us (1.17)
  waiting for transfers between devices: 320 us -> 419 us
  local copies, waits for them, and re-layouts: 71.6 us -> 94 us
    all_to_all x0 -> x1, waiting for transfers between devices: none -> 217 us  [shards(): lax.all_to_all(jnp.stack([right_env[0]] * lax.axis_size('bond')), 'bond',...]
    all_gather x1 -> x0, waiting for transfers between devices: 65.7 us -> none  [shards(): lax.all_gather(right_env[0], 'bond', axis=0, tiled=True)]
    all_gather x1, waiting for transfers between devices: 75.9 us -> 17.1 us  [shards(): current = lax.all_gather(cur_site[0], 'bond', axis=0, tiled=True)]
    all_gather x1, waiting for transfers between devices: 64.7 us -> 75.5 us  [shards(): previous = lax.all_gather(prev_site[0], 'bond', axis=2, tiled=True)]
    all_to_all x0 -> x1, local copies, waits for them, and re-layouts: none -> 10.8 us  [shards(): lax.all_to_all(jnp.stack([right_env[0]] * lax.axis_size('bond')), 'bond',...]
    another operation x24 -> x25, local copies, waits for them, and re-layouts: 27.4 us -> 35.7 us
  transfers between devices with their start and end apart: 6 -> 6, of which waited for: 4 -> 4; matrix products, arithmetic and copies ran while one was open for 8% -> 9% of each run, Pallas kernels for 0% -> 0%
where the time goes in v1:
time: 893 us; the launch traced here: 882 us
  waiting for transfers between devices  419 us (47%)
  other arithmetic  265 us (30%)
  local copies, waits for them, and re-layouts  94 us (11%)
  matrix products  73.9 us (8%)
  between operations  19.4 us (2%)
  starting transfers between devices  10.4 us (1%)
    all_to_all x1, waiting for transfers between devices, shards(): lax.all_to_all(jnp.stack([right_env[0]] * lax.axis_size('bond')), 'bond',...  217 us
    another operation x30, other arithmetic, shards(): triangle = jnp.linalg.cholesky(correlation)  173 us
    psum x1, waiting for transfers between devices, shards(): correlation = lax.psum(local_correlation, 'bond')  109 us
    another operation x3, other arithmetic, shards(): solved = jax.scipy.linalg.solve_triangular(triangle, target.T, lower=True)  86.9 us
    all_gather x1, waiting for transfers between devices, shards(): previous = lax.all_gather(prev_site[0], 'bond', axis=2, tiled=True)  75.5 us
    another operation x24, local copies, waits for them, and re-layouts  28.3 us
    another operation x14, matrix products, shards(): triangle = jnp.linalg.cholesky(correlation)  22.8 us
  transfers between devices with their start and end apart: 6, of which 4 were waited for; matrix products, arithmetic and copies ran while one was open for 9% of the time, Pallas kernels for 0%

profile of v1, /device:TPU:1, one launch (start us, length us, event | category | flops | bytes accessed | tf_op | source)
XLA Modules:
  0.0 881.8 jit_solution(12693982879315769508)
XLA Ops:
  10.2 7.3 stack.3
  17.6 7.8 all-to-all-start
  27.9 216.8 %all-to-all-done = bf16[16,64,6,1024]{3,1,2,0:T(8,128)(2,1)} async-done(((bf16[16,64,6,1024]{3,1,2,0:T(8,128)(2,1)}), bf16[16,64,6,1024]{3,1,2,0:T(8,128)(2,1)}, u32[]{:S(2)}, u32[]{:S(2)}) %all-to-all-start) | async-done | bytes 12582944 | tf_op jit(solution)/shard_map/all_to_all | solution.py:35
  244.7 10.8 %copy.56 = bf16[16,64,6,1024]{3,1,0,2:T(8,128)(2,1)} copy(bf16[16,64,6,1024]{3,1,2,0:T(8,128)(2,1)} %all-to-all-done) | data formatting | bytes 25165824 | tf_op jit(solution)/shard_map/all_to_all | solution.py:35
  255.5 17.1 %all-gather.5.cloned.1.call-done = bf16[1,1024,4,1024]{3,2,0,1:T(4,128)(2,1)} async-done(((bf16[1,64,4,1024]{3,2,0,1:T(4,128)(2,1)}), bf16[1,1024,4,1024]{3,2,0,1:T(4,128)(2,1)}) %all-gather.5.cloned.1.call-update) | async-done | bytes 8388624 | tf_op jit(solution)/shard_map/all_gather | solution.py:22
  272.5 13.8 %copy.84 = bf16[1,1024,4,1024]{1,3,2,0:T(8,128)(2,1)} copy(bf16[1,1024,4,1024]{3,2,0,1:T(4,128)(2,1)} %all-gather.5.cloned.1.call-done) | data formatting | bytes 16777216 | tf_op jit(solution)/shard_map/reshape | solution.py:25
  286.3 75.5 %all-gather.7.cloned.1.call-done = bf16[1,1024,4,1024]{1,2,0,3:T(4,128)(2,1)} async-done(((bf16[1,1024,4,64]{1,2,0,3:T(4,128)(2,1)}), bf16[1,1024,4,1024]{1,2,0,3:T(4,128)(2,1)}) %all-gather.7.cloned.1.call-update) | async-done | bytes 8388624 | tf_op jit(solution)/shard_map/all_gather | solution.py:39
  361.9 13.7 %copy.59 = bf16[1,1024,4,1024]{3,1,2,0:T(8,128)(2,1)} copy(bf16[1,1024,4,1024]{1,2,0,3:T(4,128)(2,1)} %all-gather.7.cloned.1.call-done) | data formatting | bytes 16777216 | tf_op jit(solution)/shard_map/all_gather | solution.py:39
  375.6 6.1 fusion.13
  381.7 9.4 %fusion.6 = bf16[64,4,6,1024]{3,2,1,0:T(8,128)(2,1)S(1)} fusion(f32[64,6,4,1024,1]{3,0,2,1,4:T(8,128)S(1)} %fusion.13, bf16[1,6,6,4,4]{2,4,3,1,0:T(4,128)(2,1)S(1)} %copy-done.4), kind=kOutput, calls=%fused_computation.9 | convolution fusion | flops 454557696 | bytes 9438336 | tf_op jit(solution)/shard_map/autc,uvst->asvc/dot_general | solution.py:28
  391.1 9.7 %fusion.24 = f32[64,4,1024]{2,0,1:T(8,128)} fusion(bf16[1024,6,1024,1]{2,0,1,3:T(8,128)(2,1)} %bitcast.172, bf16[64,4,6,1024]{3,2,1,0:T(8,128)(2,1)S(1)} %fusion.6), kind=kOutput, calls=%fused_computation.23 | convolution fusion | flops 3221487616 | bytes 16777216 | tf_op jit(solution)/shard_map/asvc,cvy->asy/dot_general | solution.py:31
  400.8 5.9 fusion.18
  416.6 108.7 %all-reduce.3.cloned.1.call-done = f32[1024,1024]{0,1:T(8,128)} async-done(((f32[1024,1024]{0,1:T(8,128)}), f32[1024,1024]{0,1:T(8,128)}) %all-reduce.3.cloned.1.call-update) | async-done | bytes 4194320 | tf_op jit(solution)/shard_map/psum | solution.py:51
  525.4 5.4 copy.61
  537.3 11.7 %cholesky.223 = f32[128,128]{1,0:T(8,128)S(1)} custom-call(f32[128,128]{1,0:T(8,128)S(1)} %cholesky.580), custom_call_target="Cholesky" | custom-call | tf_op jit(solution)/shard_map/jit(cholesky)/cholesky | solution.py:52
  549.0 9.8 %custom-call.63 = f32[1,128,128]{1,2,0:T(8,128)S(1)} custom-call(f32[1,128,128]{2,1,0:T(8,128)S(1)} %get-tuple-element.76), custom_call_target="InvertDiagBlocksLowerTriangular" | custom-call | tf_op jit(solution)/shard_map/jit(cholesky)/cholesky | solution.py:52
  562.6 12.1 %cholesky.244 = f32[128,128]{1,0:T(8,128)S(1)} custom-call(f32[128,128]{1,0:T(8,128)S(1)} %cholesky.584), custom_call_target="Cholesky" | custom-call | tf_op jit(solution)/shard_map/jit(cholesky)/cholesky | solution.py:52
  578.7 9.8 %custom-call.64 = f32[1,128,128]{1,2,0:T(8,128)S(1)} custom-call(f32[1,128,128]{2,1,0:T(8,128)S(1)} %get-tuple-element.73), custom_call_target="InvertDiagBlocksLowerTriangular" | custom-call | tf_op jit(solution)/shard_map/jit(cholesky)/cholesky | solution.py:52
  591.9 11.7 %cholesky.468 = f32[128,128]{1,0:T(8,128)S(1)} custom-call(f32[128,128]{1,0:T(8,128)S(1)} %cholesky.589), custom_call_target="Cholesky" | custom-call | tf_op jit(solution)/shard_map/jit(cholesky)/cholesky | solution.py:52
  604.2 9.8 %custom-call.65 = f32[1,128,128]{1,2,0:T(8,128)S(1)} custom-call(f32[1,128,128]{2,1,0:T(8,128)S(1)} %get-tuple-element.70), custom_call_target="InvertDiagBlocksLowerTriangular" | custom-call | tf_op jit(solution)/shard_map/jit(cholesky)/cholesky | solution.py:52
  617.6 11.9 %cholesky.487 = f32[128,128]{1,0:T(8,128)S(1)} custom-call(f32[128,128]{1,0:T(8,128)S(1)} %cholesky.594), custom_call_target="Cholesky" | custom-call | tf_op jit(solution)/shard_map/jit(cholesky)/cholesky | solution.py:52
  630.1 9.8 %custom-call.66 = f32[1,128,128]{1,2,0:T(8,128)S(1)} custom-call(f32[1,128,128]{2,1,0:T(8,128)S(1)} %get-tuple-element.67), custom_call_target="InvertDiagBlocksLowerTriangular" | custom-call | tf_op jit(solution)/shard_map/jit(cholesky)/cholesky | solution.py:52
  643.4 11.7 %cholesky.506 = f32[128,128]{1,0:T(8,128)S(1)} custom-call(f32[128,128]{1,0:T(8,128)S(1)} %cholesky.599), custom_call_target="Cholesky" | custom-call | tf_op jit(solution)/shard_map/jit(cholesky)/cholesky | solution.py:52
  655.7 10.0 %custom-call.67 = f32[1,128,128]{1,2,0:T(8,128)S(1)} custom-call(f32[1,128,128]{2,1,0:T(8,128)S(1)} %get-tuple-element.64), custom_call_target="InvertDiagBlocksLowerTriangular" | custom-call | tf_op jit(solution)/shard_map/jit(cholesky)/cholesky | solution.py:52
  669.1 11.7 %cholesky.526 = f32[128,128]{1,0:T(8,128)S(1)} custom-call(f32[128,128]{1,0:T(8,128)S(1)} %cholesky.604), custom_call_target="Cholesky" | custom-call | tf_op jit(solution)/shard_map/jit(cholesky)/cholesky | solution.py:52
  681.4 9.8 %custom-call.68 = f32[1,128,128]{1,2,0:T(8,128)S(1)} custom-call(f32[1,128,128]{2,1,0:T(8,128)S(1)} %get-tuple-element.61), custom_call_target="InvertDiagBlocksLowerTriangular" | custom-call | tf_op jit(solution)/shard_map/jit(cholesky)/cholesky | solution.py:52
  694.3 12.1 %cholesky.546 = f32[128,128]{1,0:T(8,128)S(1)} custom-call(f32[128,128]{1,0:T(8,128)S(1)} %cholesky.609), custom_call_target="Cholesky" | custom-call | tf_op jit(solution)/shard_map/jit(cholesky)/cholesky | solution.py:52
  707.0 9.8 %custom-call.69 = f32[1,128,128]{1,2,0:T(8,128)S(1)} custom-call(f32[1,128,128]{2,1,0:T(8,128)S(1)} %get-tuple-element.58), custom_call_target="InvertDiagBlocksLowerTriangular" | custom-call | tf_op jit(solution)/shard_map/jit(cholesky)/cholesky | solution.py:52
  719.5 11.7 %cholesky.564 = f32[128,128]{1,0:T(8,128)S(1)} custom-call(f32[128,128]{1,0:T(8,128)S(1)} %convolution_subtract_fusion.13), custom_call_target="Cholesky" | custom-call | tf_op jit(solution)/shard_map/jit(cholesky)/cholesky | solution.py:52
  741.6 6.7 fusion.8
  748.3 28.4 %while.1 = (s32[]{:T(128)}, f32[1024,1024]{1,0:T(8,128)}, s32[8,2]{0,1:T(2,128)S(1)}, f32[8,128,128]{2,1,0:T(8,128)}, s32[]{:T(128)}) while((s32[]{:T(128)}, f32[1024,1024]{1,0:T(8,128)}, s32[8,2]{0,1:T(2,128)S(1)}, f32[8,128,128]{2,1,0:T(8,128)}, s32[]{:T(128)}) %tuple.65), condition=%wide.while_cond, body=%wide.while_body.sunk | while | flops 2 | bytes 132205 | solution.py:53
  776.7 80.2 %custom-call.70 = f32[8,128,128]{1,2,0:T(8,128)} custom-call(f32[8,128,128]{2,1,0:T(8,128)} %get-tuple-element.9), custom_call_target="InvertDiagBlocksLowerTriangular" | custom-call | tf_op jit(solution)/shard_map/jit(_solve_triangular)/triangular_solve | solution.py:53
  (114 shorter events, 104.1 us)
Async XLA Ops:
  7.2 393.6 %copy-start = (bf16[1,1024,1024]{2,1,0:T(8,128)(2,1)S(1)}, bf16[1,1024,1024]{2,1,0:T(8,128)(2,1)}, u32[]{:S(2)}) copy-start(bf16[1,1024,1024]{2,1,0:T(8,128)(2,1)} %param.13) | copy-start | bytes 6291460
  7.2 265.4 %all-gather.5.cloned.1.call-start = ((), (), s32[]{:S(2)}) async-start(), calls=%async_computation.2 | async-start | bytes 8912896 | tf_op jit(solution)/shard_map/all_gather | solution.py:22
  7.9 353.9 %all-gather.7.cloned.1.call-start = ((), (), s32[]{:S(2)}) async-start(), calls=%async_computation.3 | async-start | bytes 8912896 | tf_op jit(solution)/shard_map/all_gather | solution.py:39
  17.6 7.8 copy-start.5
  17.6 227.1 %all-to-all-start = ((bf16[16,64,6,1024]{3,1,2,0:T(8,128)(2,1)}), bf16[16,64,6,1024]{3,1,2,0:T(8,128)(2,1)}, u32[]{:S(2)}, u32[]{:S(2)}) async-start(bf16[16,64,6,1024]{3,1,2,0:T(8,128)(2,1)} %stack.3), calls=%async_computation | async-start | bytes 25165824 | tf_op jit(solution)/shard_map/all_to_all | solution.py:35
  25.3 500.0 %all-reduce.3.cloned.1.call-start = ((), (), s32[]{:S(2)}) async-start(), calls=%async_computation.1 | async-start | bytes 8388608 | tf_op jit(solution)/shard_map/psum | solution.py:51
  25.4 350.2 %collective-permute-start = (bf16[64,6,1024]{2,0,1:T(8,128)(2,1)S(1)}, bf16[64,6,1024]{2,0,1:T(8,128)(2,1)}, u32[]{:S(2)}, u32[]{:S(2)}) collective-permute-start(bf16[64,6,1024]{2,0,1:T(8,128)(2,1)S(1)} %bitcast.184), channel_id=1, source_target_pairs={{240,0},{0,16},{16,32},{32,48},{48,64},{64,80},{80,96},{96,112},{1... | collective-permute-start | bytes 2359304 | tf_op jit(solution)/shard_map/ppermute | solution.py:14
  27.9 372.9 %collective-permute-start.1 = (bf16[1024,1024]{1,0:T(8,128)(2,1)}, bf16[1024,1024]{1,0:T(8,128)(2,1)}, u32[]{:S(2)}, u32[]{:S(2)}) collective-permute-start(bf16[1024,1024]{1,0:T(8,128)(2,1)} %bitcast.183), channel_id=1, source_target_pairs={{240,0},{0,16},{16,32},{32,48},{48,64},{64,80},{80,96},{96,112},{1... | collective-permute-start | bytes 6291464 | tf_op jit(solution)/shard_map/ppermute | solution.py:14
  375.6 6.1 copy-start.4
  535.2 2.0 copy-start.1
  741.5 115.3 %copy-start.2 = (f32[256,1024]{0,1:T(8,128)S(1)}, f32[256,1024]{0,1:T(8,128)}, u32[]{:S(2)}) copy-start(f32[256,1024]{0,1:T(8,128)} %copy.70) | copy-start | bytes 3145732
  856.8 7.2 copy-start.3
Sparse Core Ops, SparseCore 0:
  10.4 262.0 all-gather.4
  275.5 86.2 all-gather.6
  412.2 113.1 all-reduce.2
